TPU v7x, 256 devices: a whole 4x4x8 slice. The times are simulated.
256 devices in a mesh: req: 4 (over x), pos: 64 (over y, z, core).
Axes of the slice: x: 4, y: 4, z: 8, core: 2. Of those that a mesh axis runs over, the one named last changes fastest.
Arguments:
- hidden: bfloat16 [2048, 8192], P(('req', 'pos')), parts along dimension 0, may hold values from -6 to 6
- norm_gain: bfloat16 [8192], replicated, may hold values from 0.099609375 to 1.8984375
- w_query: bfloat16 [8192, 4096], P('pos'), may hold values from -0.0625 to 0.0625
- key_weight: bfloat16 [8192, 512], P('pos'), may hold values from -0.0625 to 0.0625
- value_weight: bfloat16 [8192, 512], P('pos'), may hold values from -0.0625 to 0.0625
- rotated_key_cache: bfloat16 [512, 128, 512], P(('req', 'pos')), parts along dimension 0
- paged_value_cache: bfloat16 [512, 128, 512], P(('req', 'pos')), parts along dimension 0, may hold values from -6 to 6
- page_map: int32 [512], P(('req', 'pos')), parts along dimension 0, may hold values from 0 to 127, each once
- selected_positions: int32 [2048], P('req'), parts along dimension 0, may hold values from 0 to 16383, as said below
Outputs:
- blended: bfloat16 [2048, 4096], P(('req', 'pos')), parts along dimension 0
- new_key_cache: bfloat16 [512, 128, 512], P(('req', 'pos')), parts along dimension 0
- new_value_cache: bfloat16 [512, 128, 512], P(('req', 'pos')), parts along dimension 0
There are 4 independent parts, one for each index of `req`. A program takes and returns all parts, laid end to end along the dimension named above; an argument that names none is the same for every part. Nothing has to cross between parts.
Inputs may be any that keep to these rules, and one draw needn't show every extreme that they name: `selected_positions`: 512 distinct positions in increasing order, all below the length of the request, which is a whole number between 5 and 16 of documents of 1024 tokens; the first and the last position of the request are always selected, and some request has 16 documents.
All inputs are finite; a program needn't handle non-finite values.
Results may differ from a plain program's by a relative error of at most 0.015.
The roundings to bfloat16 on the way count: a program that leaves them out, or rounds other values in their place, can miss the bound.
Values may be sent and summed in bfloat16 or wider, within the bound.
No kernel may reach another device: no remote copies, remote signals or barrier semaphores. Data moves between devices by JAX's collectives and lax.ppermute only.
A program may use at most 128 MiB of HBM per device.

v0:
```python
import jax
import jax.numpy as jnp
from jax import lax
from jax.sharding import PartitionSpec as P

QUERY_HEADS = 32
KEY_VALUE_HEADS = 4
HEAD_SIZE = 128
PAGE_TOKENS = 128


def apply_rotation(values, positions, heads):
    count = values.shape[0]
    width = values.shape[1] // heads
    half = width // 2
    shaped = values.reshape(count, heads, width)
    frequency = 500000.0 ** (-(jnp.arange(half, dtype=jnp.float32) * 2.0 / width))
    angles = positions.astype(jnp.float32)[:, None] * frequency[None, :]
    cosine = jnp.cos(angles)[:, None, :]
    sine = jnp.sin(angles)[:, None, :]
    first = shaped[..., :half]
    second = shaped[..., half:]
    joined = jnp.concatenate(
        [first * cosine - second * sine, second * cosine + first * sine], axis=-1
    )
    return joined.reshape(count, heads * width)


def on_device(
    hidden,
    norm_gain,
    w_query,
    key_weight,
    value_weight,
    rotated_key_cache,
    paged_value_cache,
    page_map,
    selected_positions,
):
    device_index = lax.axis_index("pos")
    row_count = hidden.shape[0]
    selected_rows = selected_positions.shape[0]
    query_columns = w_query.shape[1]
    key_value_columns = key_weight.shape[1]
    group_size = QUERY_HEADS // KEY_VALUE_HEADS
    factor = HEAD_SIZE ** (-0.5)
    values = hidden.astype(jnp.float32)
    meansq = jnp.mean(values * values, axis=-1, keepdims=True)
    normalized_rows = (values * lax.rsqrt(meansq + 1e-05) * norm_gain.astype(jnp.float32)).astype(
        jnp.bfloat16
    )
    columns = lax.all_to_all(normalized_rows, "pos", split_axis=1, concat_axis=0, tiled=True)
    combined_rows = lax.psum_scatter(
        jnp.concatenate(
            [
                jnp.dot(columns, w_query, preferred_element_type=jnp.float32),
                jnp.dot(columns, key_weight, preferred_element_type=jnp.float32),
                jnp.dot(columns, value_weight, preferred_element_type=jnp.float32),
            ],
            axis=1,
        ),
        "pos",
        scatter_dimension=0,
        tiled=True,
    )
    request_positions = lax.dynamic_slice_in_dim(
        selected_positions, device_index * row_count, row_count, 0
    )
    fresh_query = apply_rotation(
        combined_rows[:, :query_columns], request_positions, QUERY_HEADS
    ).astype(jnp.bfloat16)
    recomputed_key = apply_rotation(
        combined_rows[:, query_columns : query_columns + key_value_columns],
        request_positions,
        KEY_VALUE_HEADS,
    ).astype(jnp.bfloat16)
    recomputed_value = combined_rows[:, query_columns + key_value_columns :].astype(jnp.bfloat16)
    query_matrix, all_key, all_value = (
        lax.all_gather(fresh_query, "pos", axis=0, tiled=True),
        lax.all_gather(recomputed_key, "pos", axis=0, tiled=True),
        lax.all_gather(recomputed_value, "pos", axis=0, tiled=True),
    )
    slots = rotated_key_cache.shape[0]
    local_rows = slots * PAGE_TOKENS
    key_pos = (
        page_map[:, None] * PAGE_TOKENS + jnp.arange(PAGE_TOKENS, dtype=jnp.int32)[None, :]
    ).reshape(local_rows)
    matches = key_pos[:, None] == selected_positions[None, :]
    one_hot = matches.astype(jnp.bfloat16)
    placed = jnp.dot(
        one_hot, jnp.concatenate([all_key, all_value], axis=1), preferred_element_type=jnp.float32
    ).astype(jnp.bfloat16)
    touched = jnp.any(matches, axis=1)[:, None]
    local_key = jnp.where(
        touched,
        placed[:, :key_value_columns],
        rotated_key_cache.reshape(local_rows, key_value_columns),
    )
    local_value = jnp.where(
        touched,
        placed[:, key_value_columns:],
        paged_value_cache.reshape(local_rows, key_value_columns),
    )
    query_split_heads = query_matrix.reshape(selected_rows, KEY_VALUE_HEADS, group_size, HEAD_SIZE)
    counted = key_pos[None, None, :] <= selected_positions[:, None, None]
    score_list = []
    for head_index in range(KEY_VALUE_HEADS):
        head_keys = local_key[:, head_index * HEAD_SIZE : (head_index + 1) * HEAD_SIZE]
        scores = (
            jnp.einsum(
                "sgd,kd->sgk",
                query_split_heads[:, head_index],
                head_keys,
                preferred_element_type=jnp.float32,
            )
            * factor
        )
        score_list.append(scores)
    local_top = jnp.stack(
        [jnp.max(jnp.where(counted, item, -jnp.inf), axis=-1) for item in score_list], axis=1
    )
    global_top = lax.pmax(local_top.astype(jnp.bfloat16), "pos").astype(local_top.dtype)
    sums = []
    totals = []
    for head_index in range(KEY_VALUE_HEADS):
        weights = jnp.where(
            counted, jnp.exp(score_list[head_index] - global_top[:, head_index][..., None]), 0.0
        )
        totals.append(jnp.sum(weights, axis=-1))
        head_values = local_value[:, head_index * HEAD_SIZE : (head_index + 1) * HEAD_SIZE]
        sums.append(
            jnp.einsum(
                "sgk,kd->sgd",
                weights.astype(jnp.bfloat16),
                head_values,
                preferred_element_type=jnp.float32,
            )
        )
    summed_all = jnp.stack(sums, axis=1).reshape(selected_rows, QUERY_HEADS * HEAD_SIZE)
    total_all = jnp.stack(totals, axis=1).reshape(selected_rows, QUERY_HEADS)
    summed_own, total_own = (
        lax.psum_scatter(summed_all, "pos", scatter_dimension=0, tiled=True),
        lax.psum_scatter(total_all, "pos", scatter_dimension=0, tiled=True),
    )
    result = summed_own.reshape(row_count, QUERY_HEADS, HEAD_SIZE) / total_own[..., None]
    blended = result.reshape(row_count, QUERY_HEADS * HEAD_SIZE).astype(jnp.bfloat16)
    return (
        blended,
        local_key.reshape(slots, PAGE_TOKENS, key_value_columns),
        local_value.reshape(slots, PAGE_TOKENS, key_value_columns),
    )


def solution(mesh):
    return jax.shard_map(
        on_device,
        mesh=mesh,
        in_specs=(
            P(("req", "pos"), None),
            P(),
            P("pos", None),
            P("pos", None),
            P("pos", None),
            P(("req", "pos"), None, None),
            P(("req", "pos"), None, None),
            P(("req", "pos")),
            P("req"),
        ),
        out_specs=(
            P(("req", "pos"), None),
            P(("req", "pos"), None, None),
            P(("req", "pos"), None, None),
        ),
        check_vma=False,
    )
```

profile of v0, /device:TPU:2, one launch (start us, length us, event | category | flops | bytes accessed | tf_op | source)
XLA Modules:
  0.0 897.4 jit_solution(11979664128685601671)
XLA Ops:
  8.0 1.1 fusion.52
  9.1 1.0 fusion.57
  10.1 22.2 %all_to_all.19 = bf16[8,64,128]{2,0,1:T(8,128)(2,1)S(1)} all-to-all(bf16[8,64,128]{2,0,1:T(8,128)(2,1)S(1)} %fusion.57), channel_id=1, replica_groups=mesh['req'=4,'pos'=64] {'pos'}, dimensions={1} | all-to-all | bytes 262144 | tf_op jit(solution)/shard_map/all_to_all | solution.py:52
  32.4 1.2 fusion.63
  34.2 5.6 pad_maximum_fusion
  40.7 151.2 %reduce-scatter.4.cloned.1.call-done = f32[8,5120]{1,0:T(8,128)} async-done(((f32[512,5120]{1,0:T(8,128)}), f32[8,5120]{1,0:T(8,128)}) %reduce-scatter.4.cloned.1.call-update) | async-done | bytes 163856 | tf_op jit(solution)/shard_map/reduce_scatter | solution.py:53
  191.8 0.9 slice_bitcast_fusion.8
  195.7 48.7 %all_gather.10 = bf16[512,512]{1,0:T(8,128)(2,1)S(1)} all-gather(bf16[8,512]{1,0:T(8,128)(2,1)S(1)} %maximum_bitcast_fusion.2), channel_id=1, replica_groups=mesh['req'=4,'pos'=64] {'pos'}, dimensions={0}, use_global_device_ids=true | all-gather | bytes 532480 | tf_op jit(solution)/shard_map/all_gather | solution.py:80
  244.4 48.6 %all_gather.11 = bf16[512,512]{1,0:T(8,128)(2,1)S(1)} all-gather(bf16[8,512]{1,0:T(8,128)(2,1)S(1)} %slice.167), channel_id=1, replica_groups=mesh['req'=4,'pos'=64] {'pos'}, dimensions={0}, use_global_device_ids=true | all-gather | bytes 532480 | tf_op jit(solution)/shard_map/all_gather | solution.py:81
  293.7 6.7 copy.57
  300.4 2.1 fusion.45
  304.9 4.4 select_reduce_fusion.3
  309.2 248.9 %pmax.7 = bf16[512,4,8]{0,2,1:T(8,128)(2,1)S(1)} all-reduce(bf16[512,4,8]{0,2,1:T(8,128)(2,1)S(1)} %pad_maximum_fusion.2), channel_id=1, replica_groups=mesh['req'=4,'pos'=64] {'pos'}, use_global_device_ids=true, to_apply=%region_7.8 | all-reduce | flops 16384 | bytes 65536 | tf_op jit(solution)/shard_map/pmax | solution.py:122
  558.1 3.3 fusion.35
  561.6 2.3 fusion.38
  563.9 2.3 fusion.32
  566.2 1.5 copy-done.3
  567.6 3.7 fusion
  571.4 2.3 fusion.41
  574.4 5.7 pad_maximum_fusion.1
  580.1 9.0 copy.70
  591.2 144.8 %all-reduce.3.cloned.1.call-done = f32[512,32]{0,1:T(8,128)} async-done(((f32[512,32]{0,1:T(8,128)}), f32[512,32]{0,1:T(8,128)}) %all-reduce.3.cloned.1.call-update) | async-done | bytes 65552
  736.8 152.4 %reduce-scatter.6.cloned.1.call-done = f32[8,4096]{1,0:T(8,128)} async-done(((f32[512,4096]{1,0:T(8,128)}), f32[8,4096]{1,0:T(8,128)}) %reduce-scatter.6.cloned.1.call-update) | async-done | bytes 131088 | tf_op jit(solution)/shard_map/reduce_scatter | solution.py:142
  889.2 1.6 fusion.58
  (73 shorter events, 11.2 us)
Async XLA Ops:
  7.2 25.2 %copy-start = (bf16[128,4096]{1,0:T(8,128)(2,1)S(1)}, bf16[128,4096]{1,0:T(8,128)(2,1)}, u32[]{:S(2)}) copy-start(bf16[128,4096]{1,0:T(8,128)(2,1)} %param.11) | copy-start | bytes 3145732
  7.2 184.7 %reduce-scatter.4.cloned.1.call-start = ((), (), s32[]{:S(2)}) async-start(), calls=%async_computation.3 | async-start | bytes 10649600 | tf_op jit(solution)/shard_map/reduce_scatter | solution.py:53
  32.3 1.3 copy-start.14
  32.4 1.5 copy-start.15
  39.8 0.7 copy-start.16
  39.8 153.9 %copy-start.17 = (s32[2]{0:T(128)S(1)}, s32[2]{0:T(128)}, u32[]{:S(2)}) copy-start(s32[2]{0:T(128)} %param.16) | copy-start | bytes 28
  39.8 253.6 %copy-start.12 = (bf16[2,128,512]{2,1,0:T(8,128)(2,1)S(1)}, bf16[2,128,512]{2,1,0:T(8,128)(2,1)}, u32[]{:S(2)}) copy-start(bf16[2,128,512]{2,1,0:T(8,128)(2,1)} %param.15) | copy-start | bytes 786436
  39.8 253.6 %copy-start.13 = (bf16[2,128,512]{2,1,0:T(8,128)(2,1)S(1)}, bf16[2,128,512]{2,1,0:T(8,128)(2,1)}, u32[]{:S(2)}) copy-start(bf16[2,128,512]{2,1,0:T(8,128)(2,1)} %param.14) | copy-start | bytes 786436
  39.9 253.8 %all-gather.2.cloned.1.call-start = ((), (), s32[]{:S(2)}) async-start(), calls=%async_computation.4 | async-start | bytes 4259840 | tf_op jit(solution)/shard_map/all_gather | solution.py:79
  193.6 542.4 %all-reduce.3.cloned.1.call-start = ((), (), s32[]{:S(2)}) async-start(), calls=%async_computation.6 | async-start | bytes 131072
  293.6 10.7 %copy-start.11 = (bf16[256,512]{1,0:T(8,128)(2,1)}, bf16[256,512]{1,0:T(8,128)(2,1)S(1)}, u32[]{:S(2)}) copy-start(bf16[256,512]{1,0:T(8,128)(2,1)S(1)} %get-tuple-element.12) | copy-start | bytes 786436
  293.6 277.7 %copy-start.10 = (bf16[256,512]{1,0:T(8,128)(2,1)}, bf16[256,512]{1,0:T(8,128)(2,1)S(1)}, u32[]{:S(2)}) copy-start(bf16[256,512]{1,0:T(8,128)(2,1)S(1)} %get-tuple-element.11) | copy-start | bytes 786436
  300.4 2.5 copy-start.9
  302.9 2.0 copy-start.4
  303.6 5.6 copy-start.6
  304.9 4.4 copy-start.2
  558.1 3.4 copy-start.5
  561.4 2.4 copy-start.8
  561.6 4.6 copy-start.7
  563.9 3.8 copy-start.3
  574.4 314.8 %reduce-scatter.6.cloned.1.call-start = ((), (), s32[]{:S(2)}) async-start(), calls=%async_computation.5 | async-start | bytes 8519680 | tf_op jit(solution)/shard_map/reduce_scatter | solution.py:142
  589.1 301.8 %copy-start.1 = (bf16[128,4096]{1,0:T(8,128)(2,1)S(1)}, bf16[128,4096]{1,0:T(8,128)(2,1)}, u32[]{:S(2)}) copy-start(bf16[128,4096]{1,0:T(8,128)(2,1)} %param.11) | copy-start | bytes 3145732
  589.1 0.8 copy-start.18
Sparse Core Ops, SparseCore 0:
  40.0 151.8 reduce-scatter.3
  195.6 77.4 all-gather.1
  574.5 161.4 all-reduce.2
  740.6 148.5 reduce-scatter.5
where the time goes:
time: 898 us; the launch traced here: 897 us
  waiting for transfers between devices  449 us (50%)
  blocking collectives  368 us (41%)
  local copies, waits for them, and re-layouts  23.4 us (3%)
  other arithmetic  22 us (2%)
  matrix products  20.3 us (2%)
  between operations  14.7 us (2%)
    pmax x1, blocking collectives, on_device(): lax.pmax(local_top.astype(jnp.bfloat16), 'pos').astype(local_top.dtype)  249 us
    reduce_scatter x1, waiting for transfers between devices, on_device(): lax.psum_scatter(summed_all, 'pos', scatter_dimension=0, tiled=True)  152 us
    reduce_scatter x1, waiting for transfers between devices, on_device(): lax.psum_scatter(jnp.concatenate([jnp.dot(columns, w_query, preferred_ele...  151 us
    unnamed x5, waiting for transfers between devices  145 us
    all_gather x1, blocking collectives, on_device(): lax.all_gather(recomputed_key, 'pos', axis=0, tiled=True)  48.7 us
    all_gather x1, blocking collectives, on_device(): lax.all_gather(recomputed_value, 'pos', axis=0, tiled=True)  48.6 us
    all_to_all x1, blocking collectives, on_device(): lax.all_to_all(normalized_rows, 'pos', split_axis=1, concat_axis=0, tiled...  22.2 us
  transfers between devices with their start and end apart: 4, of which 3 were waited for; matrix products, arithmetic and copies ran while one was open for 2% of the time, Pallas kernels for 0%

commit v1 on v0

v1 whole, which is shorter than its diff:
```python
import functools

import jax
import jax.numpy as jnp
from jax import lax
from jax.experimental import pallas as pl
from jax.experimental.pallas import tpu as pltpu
from jax.sharding import Mesh, PartitionSpec as P

KEY_VALUE_HEADS = 4
GROUP = 8
W = 128
NY, NZ, NC = 4, 8, 2
ROWS = 256
OWN = 32
QCOLS = GROUP * W
COLS = QCOLS + 2 * W
EXTRA = 5 * W
STAT = 16
FAR_PAGE = 1024.0
LOWEST = -3.3e38
BF = jnp.bfloat16
F32 = jnp.float32
tie = lax.optimization_barrier
VMEM = pl.BlockSpec(memory_space=pltpu.VMEM)
ANY = pl.BlockSpec(memory_space=pl.ANY)
SMEM = pl.BlockSpec(memory_space=pltpu.SMEM)


def call(kernel, name, out_shape, specs, *operands, flops=0):
    return pl.pallas_call(
        kernel,
        grid=(1,),
        in_specs=specs,
        out_specs=jax.tree.map(lambda _: VMEM, out_shape),
        out_shape=out_shape,
        compiler_params=pltpu.CompilerParams(vmem_limit_bytes=56 * 1024 * 1024),
        cost_estimate=pl.CostEstimate(flops=flops, bytes_accessed=2_000_000, transcendentals=0),
        name=name,
    )(*operands)


def shaped(*shape, dtype=BF):
    return jax.ShapeDtypeStruct(shape, dtype)


def lanes(head):
    return pl.ds(pl.multiple_of(head * W, W), W)


def pass_kernel(*refs):
    pass


def pass_on(parts, flops):
    return pl.pallas_call(
        pass_kernel,
        in_specs=[ANY] * len(parts),
        out_specs=[ANY] * len(parts),
        out_shape=[shaped(*part.shape) for part in parts],
        input_output_aliases={i: i for i in range(len(parts))},
        cost_estimate=pl.CostEstimate(flops=flops, bytes_accessed=1_000, transcendentals=0),
        compiler_params=pltpu.CompilerParams(vmem_limit_bytes=56 * 1024 * 1024),
        name="pass_on",
    )(*parts)


def replaced_rows(pages_ref, selected):
    row = lax.broadcasted_iota(jnp.int32, (ROWS, 1), 0)
    page = jnp.where(row < W, pages_ref[0], pages_ref[1])
    pos = page * W + lax.rem(row, W)
    return jnp.max(jnp.where(pos == selected, 1.0, 0.0), axis=1, keepdims=True)


def replaced_rows(pages_ref, selected):
    row = lax.broadcasted_iota(jnp.int32, (ROWS, 1), 0)
    page = jnp.where(row < W, pages_ref[0], pages_ref[1])
    pos = page * W + lax.rem(row, W)
    return jnp.max(jnp.where(pos == selected, 1.0, 0.0), axis=1, keepdims=True)


def norm_kernel(hidden_ref, gain_ref, out_ref):
    values = hidden_ref[...].astype(F32)
    meansq = jnp.mean(values * values, axis=-1, keepdims=True)
    normed = (values * lax.rsqrt(meansq + 1e-05) * gain_ref[...].astype(F32)).astype(BF)
    for z in range(NZ):
        rows = jnp.concatenate([normed[:, (y * NZ + z) * NC * W : (y * NZ + z + 1) * NC * W] for y in range(NY)], 1)
        for y in range(NY):
            out_ref[y * NZ + z] = rows


def weights_kernel(place_ref, wq_ref, wk_ref, wv_ref, *out_refs):
    for s, out in enumerate(out_refs):
        head = lax.rem(place_ref[0] + s, NY)
        out[:, :QCOLS] = wq_ref[:, pl.ds(pl.multiple_of(head * QCOLS, QCOLS), QCOLS)]
        out[:, QCOLS : QCOLS + W] = wk_ref[:, lanes(head)]
        out[:, QCOLS + W :] = wv_ref[:, lanes(head)]


def blocks_kernel(place_ref, pages_ref, selected_ref, key_ref, value_ref, *out_refs):
    hit = jnp.broadcast_to(replaced_rows(pages_ref, selected_ref[...]), (ROWS, W))
    row = lax.broadcasted_iota(jnp.int32, (W, W), 0)
    meta = jnp.zeros((W, W), F32)
    for p in range(2):
        page = pages_ref[p].astype(F32)
        far = jnp.where(hit[p * W : (p + 1) * W].T[:1] > 0.5, FAR_PAGE, page)
        meta = jnp.where(row == p, far, jnp.where(row == 2 + p, page, meta))
    meta = meta.astype(BF)
    for s, out in enumerate(out_refs):
        at = lanes(lax.rem(place_ref[0] + s, NY))
        for p in range(2):
            out[:, p * W : (p + 1) * W] = key_ref[p, :, at]
            out[:, (2 + p) * W : (3 + p) * W] = value_ref[p, :, at]
        out[:, 4 * W :] = meta


def join_kernel(*refs):
    for s, part in enumerate(refs[:-1]):
        refs[-1][s * W : (s + 1) * W, :] = part[...]


def project_kernel(place_ref, normed_ref, *refs):
    weight_refs, out_ref = refs[:-1], refs[-1]
    y, c = place_ref[0], place_ref[1]
    parts = []
    for o in range(NC):
        core = c if o == 0 else 1 - c
        for s in range(NY):
            block = lax.rem(y + NY - s, NY) * NC + core
            parts.append(normed_ref[:, :, :, lanes(block)].astype(F32))
    rows = []
    for z in range(NZ):
        for u in range(NY):
            rows.append(jnp.concatenate([part[u, z] for part in parts], axis=1))
    left = jnp.concatenate(rows, axis=0).astype(BF)
    right = jnp.concatenate([ref[...] for ref in weight_refs], axis=0)
    out = jnp.dot(left, right, preferred_element_type=F32).astype(BF)
    for z in range(NZ):
        out_ref[z] = out[z * OWN : (z + 1) * OWN]


def rotate_kernel(partial_ref, cos_ref, sin_ref, out_ref, fresh_ref):
    def total(lo):
        value = partial_ref[0, :, lo : lo + W].astype(F32)
        for z in range(1, NZ):
            value += partial_ref[z, :, lo : lo + W].astype(F32)
        return value

    def rotated(value):
        return (value * cos_ref[...] + pltpu.roll(value, W // 2, 1) * sin_ref[...]).astype(BF)

    pieces = [rotated(total(head * W)) for head in range(GROUP + 1)] + [total(QCOLS + W).astype(BF)]
    for k, piece in enumerate(pieces):
        for a in range(NZ):
            out_ref[a, :, k * W : (k + 1) * W] = piece
    fresh_ref[:, :W] = pieces[GROUP]
    fresh_ref[:, W:] = pieces[GROUP + 1]


def score(query, keys):
    return lax.dot_general(query, keys, (((1,), (1,)), ((), ())), preferred_element_type=F32)


def attend_kernel(packed_ref, token_pos_ref, fresh_ref, fresh_c_ref, fresh_pos_ref, *refs):
    block_refs, out_ref = refs[:-1], refs[-1]
    factor = W**-0.5
    lane = lax.broadcasted_iota(jnp.int32, (1, W), 1).astype(F32)
    keys, values, pos = [], [], []
    for ref in block_refs:
        for s in range(NY):
            meta = ref[s * W : s * W + 16, 4 * W :].astype(F32)
            for p in range(2):
                keys.append(ref[s * W : (s + 1) * W, p * W : (p + 1) * W])
                values.append(ref[s * W : (s + 1) * W, (2 + p) * W : (3 + p) * W])
                pos.append(meta[p : p + 1] * W + lane)
    keys, values, pos = jnp.concatenate(keys, 0), jnp.concatenate(values, 0), jnp.concatenate(pos, 1)
    fresh = jnp.concatenate([fresh_ref[...], fresh_c_ref[...]], 0)
    count = NZ * OWN
    token_pos = jnp.concatenate([token_pos_ref[...]] * 2, 0)
    fresh_pos = fresh_pos_ref[...]

    def scores_of(pair):
        query = [packed_ref[a, :, h * W : (h + 1) * W] for h in (2 * pair, 2 * pair + 1) for a in range(NZ)]
        query = jnp.concatenate(query, 0)
        return score(query, keys), score(query, fresh[:, :W])

    stat_lane = lax.broadcasted_iota(jnp.int32, (count, W), 1)
    packed = jnp.zeros((count, W), F32)
    ahead = scores_of(0)
    for pair in range(GROUP // 2):
        now, now_fresh = ahead
        if pair + 1 < GROUP // 2:
            ahead = scores_of(pair + 1)
        now = jnp.where(pos <= token_pos, now * factor, -jnp.inf)
        now_fresh = jnp.where(fresh_pos <= token_pos, now_fresh * factor, -jnp.inf)
        top = jnp.maximum(jnp.max(now, axis=1, keepdims=True), jnp.max(now_fresh, axis=1, keepdims=True))
        top = jnp.maximum(top, LOWEST)
        weights, fresh_weights = jnp.exp(now - top), jnp.exp(now_fresh - top)
        total = jnp.sum(weights, axis=1, keepdims=True) + jnp.sum(fresh_weights, axis=1, keepdims=True)
        acc = jnp.dot(weights.astype(BF), values, preferred_element_type=F32)
        acc += jnp.dot(fresh_weights.astype(BF), fresh[:, W:], preferred_element_type=F32)
        some = total > 0.0
        safe = jnp.where(some, total, 1.0)
        result = acc * jnp.where(some, 1.0 / safe, 0.0)
        spread = jnp.where(some, top + jnp.log(safe), LOWEST)
        for k in range(2):
            head = 2 * pair + k
            packed = jnp.where(stat_lane // STAT == head, spread[k * count : (k + 1) * count], packed)
            for a in range(NZ):
                for u in range(NY):
                    at = k * count + (a * NY + u) * 8
                    out_ref[u * NZ + a, :, head * W : (head + 1) * W] = result[at : at + 8].astype(BF)
    high = packed.astype(BF).astype(F32)
    middle = (packed - high).astype(BF).astype(F32)
    which = lax.rem(stat_lane, STAT)
    packed = jnp.where(which == 0, high, jnp.where(which == 1, middle, packed - high - middle))
    for a in range(NZ):
        for u in range(NY):
            at = (a * NY + u) * 8
            out_ref[u * NZ + a, :, QCOLS:] = packed[at : at + 8].astype(BF)


def merge_kernel(parts_ref, out_ref):
    for u in range(NY):
        stats = [parts_ref[u * NZ + a, :, QCOLS:].astype(F32) for a in range(NZ)]
        spread = [s + pltpu.roll(s, W - 1, 1) + pltpu.roll(s, W - 2, 1) for s in stats]
        top = functools.reduce(jnp.maximum, spread)
        share = [jnp.exp(v - top) for v in spread]
        total = functools.reduce(jnp.add, share)
        share = [v / total for v in share]
        for head in range(GROUP):
            at = head * STAT
            value = jnp.zeros((8, W), F32)
            for a in range(NZ):
                value += share[a][:, at : at + 1] * parts_ref[u * NZ + a, :, head * W : (head + 1) * W].astype(F32)
            out_ref[:, u * QCOLS + head * W : u * QCOLS + (head + 1) * W] = value.astype(BF)


def place_kernel(packed_ref, other_ref, fresh_pos_ref, *refs):
    block_refs, out_refs = refs[:NY], refs[NY:]
    fresh = jnp.concatenate([ref[a, :, QCOLS:] for ref in (packed_ref, other_ref) for a in range(NZ)], 0)
    row = lax.broadcasted_iota(jnp.int32, (ROWS, 1), 0)
    offset = lax.rem(row, W).astype(F32)
    for block, out in zip(block_refs, out_refs):
        meta = block[:16, 4 * W :].astype(F32)
        pos = jnp.where(row < W, meta[2:3, :1], meta[3:4, :1]) * W + offset
        one_hot = jnp.where(pos == fresh_pos_ref[...], 1.0, 0.0).astype(BF)
        out[...] = jnp.dot(one_hot, fresh, preferred_element_type=F32).astype(BF)


def caches_kernel(place_ref, pages_ref, selected_ref, key_ref, value_ref, *refs):
    placed_refs, (new_key_ref, new_value_ref) = refs[:NY], refs[NY:]
    hit = replaced_rows(pages_ref, selected_ref[...]) > 0.5
    for s, placed in enumerate(placed_refs):
        at = lanes(lax.rem(place_ref[0] + s, NY))
        for p in range(2):
            rows = slice(p * W, (p + 1) * W)
            new_key_ref[p, :, at] = jnp.where(hit[rows], placed[rows, :W].astype(F32), key_ref[p, :, at].astype(F32)).astype(BF)
            new_value_ref[p, :, at] = jnp.where(hit[rows], placed[rows, W:].astype(F32), value_ref[p, :, at].astype(F32)).astype(BF)


def shift(values, axis, size, step):
    return lax.ppermute(values, axis, [(i, (i + step) % size) for i in range(size)])


def swap(values, axis):
    return shift(values, axis, 2, 1)


def exchange(values, axis):
    return lax.all_to_all(values, axis, split_axis=0, concat_axis=0, tiled=True)


def on_device(hidden, norm_gain, w_query, key_weight, value_weight, key_cache, value_cache, page_map, selected):
    y, z, c = (lax.axis_index(name) for name in ("y", "z", "c"))
    place = jnp.stack([y, c]).astype(jnp.int32)
    sel = selected.astype(F32).reshape(NY, NZ, NC, 8)
    selected_row = selected[None, :]

    sent = call(
        weights_kernel, "weights", [shaped(W, COLS)] * NY, [SMEM] + [VMEM] * 3, place, w_query, key_weight, value_weight
    )
    hidden, sent = tie((hidden, sent))
    w_own = [part if s == 0 else shift(part, "y", NY, s) for s, part in enumerate(sent)]

    normed = call(norm_kernel, "norm", shaped(NY * NZ, 8, NY * NC * W), [VMEM] * 2, hidden, norm_gain[None, :])
    normed, selected_row = tie((normed, selected_row))
    normed = exchange(normed, ("y", "z"))
    w_own = pass_on(w_own, 40_000_000_000)
    w_other = [swap(part, "c") for part in w_own]

    blocks = call(
        blocks_kernel,
        "blocks",
        [shaped(W, EXTRA)] * NY,
        [SMEM, SMEM] + [VMEM] * 3,
        place,
        page_map,
        selected_row,
        key_cache,
        value_cache,
    )
    blocks = [part if s == 0 else shift(part, "y", NY, s) for s, part in enumerate(blocks)]
    mine = call(join_kernel, "join", shaped(NY * W, EXTRA), [VMEM] * NY, *blocks)

    partial = call(
        project_kernel,
        "project",
        shaped(NZ, OWN, COLS),
        [SMEM] + [VMEM] * 9,
        place,
        normed.reshape(NY, NZ, 8, -1),
        *w_own,
        *w_other,
        flops=700_000_000,
    )
    partial = exchange(partial, "z")
    cached = [mine, swap(mine, "c")]

    group = lambda core: lax.dynamic_index_in_dim(sel, core, 2, keepdims=False).transpose(1, 0, 2).reshape(NZ, OWN)
    groups = [group(c), group(1 - c)]
    here = lambda pos: lax.dynamic_index_in_dim(pos, z, 0, keepdims=False)
    half = W // 2
    frequency = 500000.0 ** (-(jnp.arange(half, dtype=F32) * 2.0 / W))
    angles = here(groups[0])[:, None] * frequency[None, :]
    cosine, sine = jnp.cos(angles), jnp.sin(angles)
    packed, fresh = call(
        rotate_kernel,
        "rotate",
        [shaped(NZ, OWN, COLS), shaped(OWN, 2 * W)],
        [VMEM] * 3,
        partial,
        jnp.concatenate([cosine, cosine], 1),
        jnp.concatenate([-sine, sine], 1),
    )
    packed = exchange(packed, "z")

    parts = call(
        attend_kernel,
        "attend",
        shaped(NY * NZ, 8, QCOLS + W),
        [VMEM] * 7,
        packed,
        groups[0].reshape(-1, 1),
        fresh,
        swap(fresh, "c"),
        jnp.concatenate([here(g) for g in groups])[None, :],
        *cached,
        flops=2_200_000_000,
    )
    parts = exchange(parts, ("y", "z"))
    blended = call(merge_kernel, "merge", shaped(8, NY * QCOLS), [VMEM], parts)

    placed = call(
        place_kernel,
        "place",
        [shaped(ROWS, 2 * W)] * NY,
        [VMEM] * 7,
        packed,
        swap(packed, "c"),
        jnp.concatenate([g.reshape(-1) for g in groups])[None, :],
        *blocks,
    )
    placed = [part if s == 0 else shift(part, "y", NY, NY - s) for s, part in enumerate(placed)]
    new_key, new_value = call(
        caches_kernel,
        "caches",
        [shaped(2, W, KEY_VALUE_HEADS * W)] * 2,
        [SMEM, SMEM] + [VMEM] * 7,
        place,
        page_map,
        selected_row,
        key_cache,
        value_cache,
        *placed,
    )
    return blended, new_key, new_value


def solution(mesh):
    fine = Mesh(mesh.devices.reshape(mesh.devices.shape[0], NY, NZ, NC), ("req", "y", "z", "c"))
    every = ("req", "y", "z", "c")
    pos = every[1:]
    return jax.shard_map(
        on_device,
        mesh=fine,
        in_specs=(
            P(every, None),
            P(),
            P(pos, None),
            P(pos, None),
            P(pos, None),
            P(every, None, None),
            P(every, None, None),
            P(every),
            P("req"),
        ),
        out_specs=(P(every, None), P(every, None, None), P(every, None, None)),
        check_vma=False,
    )
```

time: 898 us -> 139 us (0.15)
  waiting for transfers between devices: 449 us -> 49.4 us
  blocking collectives: 368 us -> 0 us
  starting transfers between devices: 0.16 us -> 41.8 us
  Pallas kernels: 0 us -> 32.4 us
  matrix products: 20.3 us -> 0 us
  other arithmetic: 22 us -> 2.7 us
  between operations: 14.7 us -> 0.84 us
  local copies, waits for them, and re-layouts: 23.4 us -> 10.4 us
    reduce_scatter x2 -> x0, waiting for transfers between devices: 304 us -> none  [the longest x1 152 us: on_device(): lax.psum_scatter(summed_all, 'pos', scatter_dimension=0, tiled=True)]
    pmax x1 -> x0, blocking collectives: 249 us -> none  [on_device(): lax.pmax(local_top.astype(jnp.bfloat16), 'pos').astype(local_top.dtype)]
    unnamed x5 -> x0, waiting for transfers between devices: 145 us -> none
    all_gather x2 -> x0, blocking collectives: 97.2 us -> none  [the longest x1 48.7 us: on_device(): lax.all_gather(recomputed_key, 'pos', axis=0, tiled=True)]
    pallas_call x0 -> x11, Pallas kernels: none -> 32.4 us  [the longest x10 32.4 us: call(): pl.pallas_call(kernel, grid=(1,), in_specs=specs, out_specs=jax.tree.map(...]
    all_to_all x0 -> x4, waiting for transfers between devices: none -> 26.9 us  [exchange(): return lax.all_to_all(values, axis, split_axis=0, concat_axis=0, tiled=True)]
    all_to_all x0 -> x4, starting transfers between devices: none -> 24.8 us  [exchange(): return lax.all_to_all(values, axis, split_axis=0, concat_axis=0, tiled=True)]
    ppermute x0 -> x16, waiting for transfers between devices: none -> 22.5 us  [shift(): lax.ppermute(values, axis, [(i, (i + step) % size) for i in range(size)])]
  transfers between devices with their start and end apart: 4 -> 20, of which waited for: 3 -> 13; matrix products, arithmetic and copies ran while one was open for 2% -> 3% of each run, Pallas kernels for 0% -> 8%
where the time goes in v1:
time: 139 us; the launch traced here: 137 us
  waiting for transfers between devices  49.4 us (36%)
  starting transfers between devices  41.8 us (30%)
  Pallas kernels  32.4 us (23%)
  local copies, waits for them, and re-layouts  10.4 us (7%)
  other arithmetic  2.7 us (2%)
    pallas_call x10, Pallas kernels, call(): pl.pallas_call(kernel, grid=(1,), in_specs=specs, out_specs=jax.tree.map(...  32.4 us
    all_to_all x4, waiting for transfers between devices, exchange(): return lax.all_to_all(values, axis, split_axis=0, concat_axis=0, tiled=True)  26.9 us
    all_to_all x4, starting transfers between devices, exchange(): return lax.all_to_all(values, axis, split_axis=0, concat_axis=0, tiled=True)  24.8 us
    ppermute x16, waiting for transfers between devices, shift(): lax.ppermute(values, axis, [(i, (i + step) % size) for i in range(size)])  22.5 us
    ppermute x16, starting transfers between devices, shift(): lax.ppermute(values, axis, [(i, (i + step) % size) for i in range(size)])  17 us
    unnamed x48, local copies, waits for them, and re-layouts  8.46 us
  transfers between devices with their start and end apart: 20, of which 13 were waited for; matrix products, arithmetic and copies ran while one was open for 3% of the time, Pallas kernels for 8%

profile of v1, /device:TPU:2, one launch (start us, length us, event | category | flops | bytes accessed | tf_op | source)
XLA Modules:
  0.0 137.4 jit_solution(7884580691421671932)
XLA Ops:
  1.3 2.5 %weights.1 = (bf16[128,1280]{1,0:T(8,128)(2,1)}, bf16[128,1280]{1,0:T(8,128)(2,1)}, bf16[128,1280]{1,0:T(8,128)(2,1)}, bf16[128,1280]{1,0:T(8,128)(2,1)}) custom-call(s32[2]{0:T(128)} %pad_add_fusion.place_ref, bf16[128,4096]{1,0:T(8,128)(2,1)} %wq_ref.1, bf16[128,512]{1,0:T(8,128)(2,1)} %wk_ref.1, bf16[128,512]{1,0:T(8,128)(2,1)} %wv_ref.1), custom_call_target="tpu_custom_call" | custom-call | bytes 2000000 | tf_op jit(solution)/shard_map/weights/pallas_call | solution.py:31
  5.4 2.9 %collective-permute-start.1 = (bf16[128,1280]{1,0:T(8,128)(2,1)}, bf16[128,1280]{1,0:T(8,128)(2,1)S(1)}, u32[]{:S(2)}, u32[]{:S(2)}) collective-permute-start(bf16[128,1280]{1,0:T(8,128)(2,1)} %get-tuple-element.38), channel_id=1, source_target_pairs={{0,32},{16,48},{32,0},{48,16},{1,33},{17,49},{33,1},{49,17},{2,34}... | collective-permute-start | bytes 983048 | tf_op jit(solution)/shard_map/ppermute | solution.py:263
  10.3 1.9 %norm.1 = bf16[32,8,1024]{2,1,0:T(8,128)(2,1)} custom-call(bf16[8,8192]{1,0:T(8,128)(2,1)} %hidden_ref, bf16[1,8192]{1,0:T(2,128)(2,1)} %broadcast_in_dim.14.gain_ref), custom_call_target="tpu_custom_call" | custom-call | bytes 2000000 | tf_op jit(solution)/shard_map/norm/pallas_call | solution.py:31
  12.2 9.0 %all-to-all-start = ((bf16[32,8,1024]{2,1,0:T(8,128)(2,1)}), bf16[32,8,1024]{2,1,0:T(8,128)(2,1)S(1)}, u32[]{:S(2)}, u32[]{:S(2)}) async-start(bf16[32,8,1024]{2,1,0:T(8,128)(2,1)} %norm.1), calls=%async_computation | async-start | bytes 1048576 | tf_op jit(solution)/shard_map/all_to_all | solution.py:271
  27.6 10.1 %all-to-all-done = bf16[32,8,1024]{2,1,0:T(8,128)(2,1)S(1)} async-done(((bf16[32,8,1024]{2,1,0:T(8,128)(2,1)}), bf16[32,8,1024]{2,1,0:T(8,128)(2,1)S(1)}, u32[]{:S(2)}, u32[]{:S(2)}) %all-to-all-start) | async-done | bytes 524320 | tf_op jit(solution)/shard_map/all_to_all | solution.py:271
  38.5 3.6 %project.1 = bf16[8,32,1280]{2,1,0:T(8,128)(2,1)} custom-call(s32[2]{0:T(128)} %pad_add_fusion.place_ref, bf16[4,8,8,1024]{3,2,1,0:T(8,128)(2,1)} %bitcast.17, bf16[128,1280]{1,0:T(8,128)(2,1)} %get-tuple-element.40.refs_0_, bf16[128,1280]{1,0:T(8,128)(2,1)} %get-tuple-element.41.refs_1_, bf16[128,1280]{1,0:T(8,128)(2,1)} %get-tuple-element.42.refs_2_, ...), custom_call_target="tpu_custom_call" | custom-call | flops 700000000 | bytes 2000000 | tf_op jit(solution)/shard_map/project/pallas_call | solution.py:31
  42.1 4.0 %all-to-all-start.1 = ((bf16[8,32,1280]{2,1,0:T(8,128)(2,1)}), bf16[8,32,1280]{2,1,0:T(8,128)(2,1)S(1)}, u32[]{:S(2)}, u32[]{:S(2)}) async-start(bf16[8,32,1280]{2,1,0:T(8,128)(2,1)} %project.1), calls=%async_computation.1 | async-start | bytes 1310720 | tf_op jit(solution)/shard_map/all_to_all | solution.py:271
  47.3 16.8 %all-to-all-done.1.partial_ref = bf16[8,32,1280]{2,1,0:T(8,128)(2,1)S(1)} async-done(((bf16[8,32,1280]{2,1,0:T(8,128)(2,1)}), bf16[8,32,1280]{2,1,0:T(8,128)(2,1)S(1)}, u32[]{:S(2)}, u32[]{:S(2)}) %all-to-all-start.1) | async-done | bytes 655392 | tf_op jit(solution)/shard_map/all_to_all | solution.py:271
  64.9 2.1 %rotate.1 = (bf16[8,32,1280]{2,1,0:T(8,128)(2,1)}, bf16[32,256]{1,0:T(8,128)(2,1)}) custom-call(bf16[8,32,1280]{2,1,0:T(8,128)(2,1)} %copy-done.2, f32[32,128]{1,0:T(8,128)} %get-tuple-element.62.cos_ref, f32[32,128]{1,0:T(8,128)} %get-tuple-element.63.sin_ref), custom_call_target="tpu_custom_call" | custom-call | bytes 2000000 | tf_op jit(solution)/shard_map/rotate/pallas_call | solution.py:31
  67.0 3.5 %all-to-all-start.2 = ((bf16[8,32,1280]{2,1,0:T(8,128)(2,1)}), bf16[8,32,1280]{2,1,0:T(8,128)(2,1)S(1)}, u32[]{:S(2)}, u32[]{:S(2)}) async-start(bf16[8,32,1280]{2,1,0:T(8,128)(2,1)} %get-tuple-element.44), calls=%async_computation.2 | async-start | bytes 1310720 | tf_op jit(solution)/shard_map/all_to_all | solution.py:271
  70.6 2.1 %blocks.1 = (bf16[128,640]{1,0:T(8,128)(2,1)}, bf16[128,640]{1,0:T(8,128)(2,1)}, bf16[128,640]{1,0:T(8,128)(2,1)}, bf16[128,640]{1,0:T(8,128)(2,1)}) custom-call(s32[2]{0:T(128)} %pad_add_fusion.place_ref, s32[2]{0:T(128)} %pages_ref.3, s32[1,512]{1,0:T(1,128)} %bitcast.20, bf16[2,128,512]{2,1,0:T(8,128)(2,1)} %key_ref.3, bf16[2,128,512]{2,1,0:T(8,128)(2,1)} %value_ref.3), custom_call_target="tpu_custom_call" | custom-call | bytes 2000000 | tf_op jit(solution)/shard_map/blocks/pallas_call | solution.py:31
  72.7 2.5 %collective-permute-start.10 = (bf16[128,640]{1,0:T(8,128)(2,1)}, bf16[128,640]{1,0:T(8,128)(2,1)S(1)}, u32[]{:S(2)}, u32[]{:S(2)}) collective-permute-start(bf16[128,640]{1,0:T(8,128)(2,1)} %get-tuple-element.50), channel_id=1, source_target_pairs={{0,48},{16,0},{32,16},{48,32},{1,49},{17,1},{33,17},{49,33},{2,50}... | collective-permute-start | bytes 491528 | tf_op jit(solution)/shard_map/ppermute | solution.py:263
  75.2 2.3 %collective-permute-start.9 = (bf16[128,640]{1,0:T(8,128)(2,1)}, bf16[128,640]{1,0:T(8,128)(2,1)S(1)}, u32[]{:S(2)}, u32[]{:S(2)}) collective-permute-start(bf16[128,640]{1,0:T(8,128)(2,1)} %get-tuple-element.49), channel_id=1, source_target_pairs={{0,32},{16,48},{32,0},{48,16},{1,33},{17,49},{33,1},{49,17},{2,34}... | collective-permute-start | bytes 491528 | tf_op jit(solution)/shard_map/ppermute | solution.py:263
  77.5 2.6 %collective-permute-done.10.refs_3_ = bf16[128,640]{1,0:T(8,128)(2,1)S(1)} collective-permute-done((bf16[128,640]{1,0:T(8,128)(2,1)}, bf16[128,640]{1,0:T(8,128)(2,1)S(1)}, u32[]{:S(2)}, u32[]{:S(2)}) %collective-permute-start.10) | collective-permute-done | bytes 163872 | tf_op jit(solution)/shard_map/ppermute | solution.py:263
  80.1 4.1 %collective-permute-done.8.refs_1_ = bf16[128,640]{1,0:T(8,128)(2,1)S(1)} collective-permute-done((bf16[128,640]{1,0:T(8,128)(2,1)}, bf16[128,640]{1,0:T(8,128)(2,1)S(1)}, u32[]{:S(2)}, u32[]{:S(2)}) %collective-permute-start.8) | collective-permute-done | bytes 163872 | tf_op jit(solution)/shard_map/ppermute | solution.py:263
  84.9 2.0 %join.1.refs_0_ = bf16[512,640]{1,0:T(8,128)(2,1)} custom-call(bf16[128,640]{1,0:T(8,128)(2,1)} %get-tuple-element.47.refs_0_, bf16[128,640]{1,0:T(8,128)(2,1)} %copy-done.6, bf16[128,640]{1,0:T(8,128)(2,1)} %copy-done.7, bf16[128,640]{1,0:T(8,128)(2,1)} %copy-done.5), custom_call_target="tpu_custom_call" | custom-call | bytes 2000000 | tf_op jit(solution)/shard_map/join/pallas_call | solution.py:31
  91.3 10.7 %attend.1 = bf16[32,8,1152]{2,1,0:T(8,128)(2,1)} custom-call(bf16[8,32,1280]{2,1,0:T(8,128)(2,1)} %copy-done, f32[256,1]{1,0:T(8,128)} %reshape_reshape.12.token_pos_ref, bf16[32,256]{1,0:T(8,128)(2,1)} %get-tuple-element.45.fresh_ref, bf16[32,256]{1,0:T(8,128)(2,1)} %copy-done.23, f32[1,64]{1,0:T(1,128)} %maximum_bitcast_fusion.fresh_pos_ref, ...), custom_call_target="tpu_custom_call" | custom-call | flops 2200000000 | bytes 2000000 | tf_op jit(solution)/shard_map/attend/pallas_call | solution.py:31
  102.0 8.2 %all-to-all-start.3 = ((bf16[32,8,1152]{2,1,0:T(8,128)(2,1)}), bf16[32,8,1152]{2,1,0:T(8,128)(2,1)S(1)}, u32[]{:S(2)}, u32[]{:S(2)}) async-start(bf16[32,8,1152]{2,1,0:T(8,128)(2,1)} %attend.1), calls=%async_computation.3 | async-start | bytes 1179648 | tf_op jit(solution)/shard_map/all_to_all | solution.py:271
  113.3 2.7 %place.1 = (bf16[256,256]{1,0:T(8,128)(2,1)}, bf16[256,256]{1,0:T(8,128)(2,1)}, bf16[256,256]{1,0:T(8,128)(2,1)}, bf16[256,256]{1,0:T(8,128)(2,1)}) custom-call(bf16[8,32,1280]{2,1,0:T(8,128)(2,1)} %copy-done, bf16[8,32,1280]{2,1,0:T(8,128)(2,1)} %copy-done.8, f32[1,512]{1,0:T(1,128)} %bitcast.22, bf16[128,640]{1,0:T(8,128)(2,1)} %get-tuple-element.47.refs_0_, ...), custom_call_target="tpu_custom_call" | custom-call | bytes 2000000 | tf_op jit(solution)/shard_map/place/pallas_call | solution.py:31
  115.9 3.0 %collective-permute-start.13 = (bf16[256,256]{1,0:T(8,128)(2,1)}, bf16[256,256]{1,0:T(8,128)(2,1)S(1)}, u32[]{:S(2)}, u32[]{:S(2)}) collective-permute-start(bf16[256,256]{1,0:T(8,128)(2,1)} %get-tuple-element.52), channel_id=1, source_target_pairs={{0,48},{16,0},{32,16},{48,32},{1,49},{17,1},{33,17},{49,33},{2,50}... | collective-permute-start | bytes 393224 | tf_op jit(solution)/shard_map/ppermute | solution.py:263
  120.7 7.3 %collective-permute-done.13.refs_1_ = bf16[256,256]{1,0:T(8,128)(2,1)S(1)} collective-permute-done((bf16[256,256]{1,0:T(8,128)(2,1)}, bf16[256,256]{1,0:T(8,128)(2,1)S(1)}, u32[]{:S(2)}, u32[]{:S(2)}) %collective-permute-start.13) | collective-permute-done | bytes 131104 | tf_op jit(solution)/shard_map/ppermute | solution.py:263
  128.9 2.3 %collective-permute-done.15.refs_3_ = bf16[256,256]{1,0:T(8,128)(2,1)S(1)} collective-permute-done((bf16[256,256]{1,0:T(8,128)(2,1)}, bf16[256,256]{1,0:T(8,128)(2,1)S(1)}, u32[]{:S(2)}, u32[]{:S(2)}) %collective-permute-start.15) | collective-permute-done | bytes 131104 | tf_op jit(solution)/shard_map/ppermute | solution.py:263
  131.8 2.3 %caches.1 = (bf16[2,128,512]{2,1,0:T(8,128)(2,1)}, bf16[2,128,512]{2,1,0:T(8,128)(2,1)}) custom-call(s32[2]{0:T(128)} %pad_add_fusion.place_ref, s32[2]{0:T(128)} %pages_ref.3, s32[1,512]{1,0:T(1,128)} %bitcast.21, bf16[2,128,512]{2,1,0:T(8,128)(2,1)} %key_ref.3, bf16[2,128,512]{2,1,0:T(8,128)(2,1)} %value_ref.3, ...), custom_call_target="tpu_custom_call" | custom-call | bytes 2000000 | tf_op jit(solution)/shard_map/caches/pallas_call | solution.py:31
  134.9 2.5 %merge.1 = bf16[8,4096]{1,0:T(8,128)(2,1)} custom-call(bf16[32,8,1152]{2,1,0:T(8,128)(2,1)} %copy-done.3), custom_call_target="tpu_custom_call" | custom-call | bytes 2000000 | tf_op jit(solution)/shard_map/merge/pallas_call | solution.py:31
  (94 shorter events, 25.5 us)
Async XLA Ops:
  3.8 17.4 %collective-permute-start = (bf16[128,1280]{1,0:T(8,128)(2,1)}, bf16[128,1280]{1,0:T(8,128)(2,1)S(1)}, u32[]{:S(2)}, u32[]{:S(2)}) collective-permute-start(bf16[128,1280]{1,0:T(8,128)(2,1)} %get-tuple-element.37), channel_id=1, source_target_pairs={{0,16},{16,32},{32,48},{48,0},{1,17},{17,33},{33,49},{49,1},{2,18}... | collective-permute-start | bytes 983048 | tf_op jit(solution)/shard_map/ppermute | solution.py:263
  5.4 17.6 %collective-permute-start.1 = (bf16[128,1280]{1,0:T(8,128)(2,1)}, bf16[128,1280]{1,0:T(8,128)(2,1)S(1)}, u32[]{:S(2)}, u32[]{:S(2)}) collective-permute-start(bf16[128,1280]{1,0:T(8,128)(2,1)} %get-tuple-element.38), channel_id=1, source_target_pairs={{0,32},{16,48},{32,0},{48,16},{1,33},{17,49},{33,1},{49,17},{2,34}... | collective-permute-start | bytes 983048 | tf_op jit(solution)/shard_map/ppermute | solution.py:263
  8.3 14.7 %collective-permute-start.2 = (bf16[128,1280]{1,0:T(8,128)(2,1)}, bf16[128,1280]{1,0:T(8,128)(2,1)S(1)}, u32[]{:S(2)}, u32[]{:S(2)}) collective-permute-start(bf16[128,1280]{1,0:T(8,128)(2,1)} %get-tuple-element.39), channel_id=1, source_target_pairs={{0,48},{16,0},{32,16},{48,32},{1,49},{17,1},{33,17},{49,33},{2,50}... | collective-permute-start | bytes 983048 | tf_op jit(solution)/shard_map/ppermute | solution.py:263
  12.2 25.5 %all-to-all-start = ((bf16[32,8,1024]{2,1,0:T(8,128)(2,1)}), bf16[32,8,1024]{2,1,0:T(8,128)(2,1)S(1)}, u32[]{:S(2)}, u32[]{:S(2)}) async-start(bf16[32,8,1024]{2,1,0:T(8,128)(2,1)} %norm.1), calls=%async_computation | async-start | bytes 1048576 | tf_op jit(solution)/shard_map/all_to_all | solution.py:271
  24.4 1.8 %collective-permute-start.3 = (bf16[128,1280]{1,0:T(8,128)(2,1)}, bf16[128,1280]{1,0:T(8,128)(2,1)S(1)}, u32[]{:S(2)}, u32[]{:S(2)}) collective-permute-start(bf16[128,1280]{1,0:T(8,128)(2,1)} %get-tuple-element.40.refs_0_), channel_id=1, source_target_pairs={{0,1},{1,0},{2,3},{3,2},{4,5},{5,4},{6,7},{7,6},{8,9},{9,8},{10,11... | collective-permute-start | bytes 983048 | tf_op jit(solution)/shard_map/ppermute | solution.py:263
  24.4 2.3 %collective-permute-start.4 = (bf16[128,1280]{1,0:T(8,128)(2,1)}, bf16[128,1280]{1,0:T(8,128)(2,1)S(1)}, u32[]{:S(2)}, u32[]{:S(2)}) collective-permute-start(bf16[128,1280]{1,0:T(8,128)(2,1)} %get-tuple-element.41.refs_1_), channel_id=1, source_target_pairs={{0,1},{1,0},{2,3},{3,2},{4,5},{5,4},{6,7},{7,6},{8,9},{9,8},{10,11... | collective-permute-start | bytes 983048 | tf_op jit(solution)/shard_map/ppermute | solution.py:263
  24.9 2.3 %collective-permute-start.5 = (bf16[128,1280]{1,0:T(8,128)(2,1)}, bf16[128,1280]{1,0:T(8,128)(2,1)S(1)}, u32[]{:S(2)}, u32[]{:S(2)}) collective-permute-start(bf16[128,1280]{1,0:T(8,128)(2,1)} %get-tuple-element.42.refs_2_), channel_id=1, source_target_pairs={{0,1},{1,0},{2,3},{3,2},{4,5},{5,4},{6,7},{7,6},{8,9},{9,8},{10,11... | collective-permute-start | bytes 983048 | tf_op jit(solution)/shard_map/ppermute | solution.py:263
  24.9 2.7 %collective-permute-start.6 = (bf16[128,1280]{1,0:T(8,128)(2,1)}, bf16[128,1280]{1,0:T(8,128)(2,1)S(1)}, u32[]{:S(2)}, u32[]{:S(2)}) collective-permute-start(bf16[128,1280]{1,0:T(8,128)(2,1)} %get-tuple-element.43.refs_3_), channel_id=1, source_target_pairs={{0,1},{1,0},{2,3},{3,2},{4,5},{5,4},{6,7},{7,6},{8,9},{9,8},{10,11... | collective-permute-start | bytes 983048 | tf_op jit(solution)/shard_map/ppermute | solution.py:263
  26.2 11.5 %copy-start.9 = (bf16[128,1280]{1,0:T(8,128)(2,1)}, bf16[128,1280]{1,0:T(8,128)(2,1)S(1)}, u32[]{:S(2)}) copy-start(bf16[128,1280]{1,0:T(8,128)(2,1)S(1)} %collective-permute-done.3.refs_4_) | copy-start | bytes 983044
  26.7 11.0 %copy-start.11 = (bf16[128,1280]{1,0:T(8,128)(2,1)}, bf16[128,1280]{1,0:T(8,128)(2,1)S(1)}, u32[]{:S(2)}) copy-start(bf16[128,1280]{1,0:T(8,128)(2,1)S(1)} %collective-permute-done.4.refs_5_) | copy-start | bytes 983044
  27.2 10.6 %copy-start.13 = (bf16[128,1280]{1,0:T(8,128)(2,1)}, bf16[128,1280]{1,0:T(8,128)(2,1)S(1)}, u32[]{:S(2)}) copy-start(bf16[128,1280]{1,0:T(8,128)(2,1)S(1)} %collective-permute-done.5.refs_6_) | copy-start | bytes 983044
  27.6 10.1 %copy-start.15 = (bf16[128,1280]{1,0:T(8,128)(2,1)}, bf16[128,1280]{1,0:T(8,128)(2,1)S(1)}, u32[]{:S(2)}) copy-start(bf16[128,1280]{1,0:T(8,128)(2,1)S(1)} %collective-permute-done.6.refs_7_) | copy-start | bytes 983044
  42.1 21.9 %all-to-all-start.1 = ((bf16[8,32,1280]{2,1,0:T(8,128)(2,1)}), bf16[8,32,1280]{2,1,0:T(8,128)(2,1)S(1)}, u32[]{:S(2)}, u32[]{:S(2)}) async-start(bf16[8,32,1280]{2,1,0:T(8,128)(2,1)} %project.1), calls=%async_computation.1 | async-start | bytes 1310720 | tf_op jit(solution)/shard_map/all_to_all | solution.py:271
  67.0 22.6 %all-to-all-start.2 = ((bf16[8,32,1280]{2,1,0:T(8,128)(2,1)}), bf16[8,32,1280]{2,1,0:T(8,128)(2,1)S(1)}, u32[]{:S(2)}, u32[]{:S(2)}) async-start(bf16[8,32,1280]{2,1,0:T(8,128)(2,1)} %get-tuple-element.44), calls=%async_computation.2 | async-start | bytes 1310720 | tf_op jit(solution)/shard_map/all_to_all | solution.py:271
  72.7 7.5 %collective-permute-start.10 = (bf16[128,640]{1,0:T(8,128)(2,1)}, bf16[128,640]{1,0:T(8,128)(2,1)S(1)}, u32[]{:S(2)}, u32[]{:S(2)}) collective-permute-start(bf16[128,640]{1,0:T(8,128)(2,1)} %get-tuple-element.50), channel_id=1, source_target_pairs={{0,48},{16,0},{32,16},{48,32},{1,49},{17,1},{33,17},{49,33},{2,50}... | collective-permute-start | bytes 491528 | tf_op jit(solution)/shard_map/ppermute | solution.py:263
  75.2 9.0 %collective-permute-start.8 = (bf16[128,640]{1,0:T(8,128)(2,1)}, bf16[128,640]{1,0:T(8,128)(2,1)S(1)}, u32[]{:S(2)}, u32[]{:S(2)}) collective-permute-start(bf16[128,640]{1,0:T(8,128)(2,1)} %get-tuple-element.48), channel_id=1, source_target_pairs={{0,16},{16,32},{32,48},{48,0},{1,17},{17,33},{33,49},{49,1},{2,18}... | collective-permute-start | bytes 491528 | tf_op jit(solution)/shard_map/ppermute | solution.py:263
  75.2 9.0 %collective-permute-start.9 = (bf16[128,640]{1,0:T(8,128)(2,1)}, bf16[128,640]{1,0:T(8,128)(2,1)S(1)}, u32[]{:S(2)}, u32[]{:S(2)}) collective-permute-start(bf16[128,640]{1,0:T(8,128)(2,1)} %get-tuple-element.49), channel_id=1, source_target_pairs={{0,32},{16,48},{32,0},{48,16},{1,33},{17,49},{33,1},{49,17},{2,34}... | collective-permute-start | bytes 491528 | tf_op jit(solution)/shard_map/ppermute | solution.py:263
  87.0 2.6 %collective-permute-start.11 = (bf16[512,640]{1,0:T(8,128)(2,1)}, bf16[512,640]{1,0:T(8,128)(2,1)S(1)}, u32[]{:S(2)}, u32[]{:S(2)}) collective-permute-start(bf16[512,640]{1,0:T(8,128)(2,1)} %join.1.refs_0_), channel_id=1, source_target_pairs={{0,1},{1,0},{2,3},{3,2},{4,5},{5,4},{6,7},{7,6},{8,9},{9,8},{10,11... | collective-permute-start | bytes 1966088 | tf_op jit(solution)/shard_map/ppermute | solution.py:263
  87.7 1.9 %collective-permute-start.7 = (bf16[32,256]{1,0:T(8,128)(2,1)S(1)}, bf16[32,256]{1,0:T(8,128)(2,1)S(1)}, u32[]{:S(2)}, u32[]{:S(2)}) collective-permute-start(bf16[32,256]{1,0:T(8,128)(2,1)S(1)} %copy-done.22), channel_id=1, source_target_pairs={{0,1},{1,0},{2,3},{3,2},{4,5},{5,4},{6,7},{7,6},{8,9},{9,8},{10,11... | collective-permute-start | bytes 49160 | tf_op jit(solution)/shard_map/ppermute | solution.py:263
  102.0 32.1 %all-to-all-start.3 = ((bf16[32,8,1152]{2,1,0:T(8,128)(2,1)}), bf16[32,8,1152]{2,1,0:T(8,128)(2,1)S(1)}, u32[]{:S(2)}, u32[]{:S(2)}) async-start(bf16[32,8,1152]{2,1,0:T(8,128)(2,1)} %attend.1), calls=%async_computation.3 | async-start | bytes 1179648 | tf_op jit(solution)/shard_map/all_to_all | solution.py:271
  110.2 2.2 %collective-permute-start.12 = (bf16[8,32,1280]{2,1,0:T(8,128)(2,1)S(1)}, bf16[8,32,1280]{2,1,0:T(8,128)(2,1)S(1)}, u32[]{:S(2)}, u32[]{:S(2)}) collective-permute-start(bf16[8,32,1280]{2,1,0:T(8,128)(2,1)S(1)} %copy-done.1), channel_id=1, source_target_pairs={{0,1},{1,0},{2,3},{3,2},{4,5},{5,4},{6,7},{7,6},{8,9},{9,8},{10,11... | collective-permute-start | bytes 1966088 | tf_op jit(solution)/shard_map/ppermute | solution.py:263
  115.9 12.0 %collective-permute-start.13 = (bf16[256,256]{1,0:T(8,128)(2,1)}, bf16[256,256]{1,0:T(8,128)(2,1)S(1)}, u32[]{:S(2)}, u32[]{:S(2)}) collective-permute-start(bf16[256,256]{1,0:T(8,128)(2,1)} %get-tuple-element.52), channel_id=1, source_target_pairs={{0,48},{16,0},{32,16},{48,32},{1,49},{17,1},{33,17},{49,33},{2,50}... | collective-permute-start | bytes 393224 | tf_op jit(solution)/shard_map/ppermute | solution.py:263
  119.0 9.9 %collective-permute-start.14 = (bf16[256,256]{1,0:T(8,128)(2,1)}, bf16[256,256]{1,0:T(8,128)(2,1)S(1)}, u32[]{:S(2)}, u32[]{:S(2)}) collective-permute-start(bf16[256,256]{1,0:T(8,128)(2,1)} %get-tuple-element.53), channel_id=1, source_target_pairs={{0,32},{16,48},{32,0},{48,16},{1,33},{17,49},{33,1},{49,17},{2,34}... | collective-permute-start | bytes 393224 | tf_op jit(solution)/shard_map/ppermute | solution.py:263
  119.8 11.3 %collective-permute-start.15 = (bf16[256,256]{1,0:T(8,128)(2,1)}, bf16[256,256]{1,0:T(8,128)(2,1)S(1)}, u32[]{:S(2)}, u32[]{:S(2)}) collective-permute-start(bf16[256,256]{1,0:T(8,128)(2,1)} %get-tuple-element.54), channel_id=1, source_target_pairs={{0,16},{16,32},{32,48},{48,0},{1,17},{17,33},{33,49},{49,1},{2,18}... | collective-permute-start | bytes 393224 | tf_op jit(solution)/shard_map/ppermute | solution.py:263
  (20 other events, 42.0 us)
